TPU v7x, 512 devices: a whole 4x4x16 slice. The times are simulated.
512 devices in a mesh: band: 64 (over z_lo, y, core), grid: 8 (over x, z_hi).
Axes of the slice: x: 4, y: 4, z: 16 (z_hi: 2, z_lo: 8; z = z_hi * 8 + z_lo), core: 2. Of those that a mesh axis runs over, the one named last changes fastest.
Arguments:
- bands: float32 [256, 80, 6400], P('band', 'grid'), may hold values from -6 to 6
- pair_list: int32 [64, 2, 1, 2], P('band'), may hold values from 0 to 3
Outputs:
- exchange_action: float32 [256, 80, 6400], P('band', 'grid')
Inputs may be any that keep to these rules, and one draw needn't show every extreme that they name: `pair_list`: band indices within a block.
All inputs are finite; a program needn't handle non-finite values.
Results may differ from a plain program's by a relative error of at most 0.0001.
Values sent between devices are 32-bit elements; how exact they have to be, the bound alone decides.
A program may use at most 64 MiB of HBM per device.

v0:
```python
import math

import jax
import jax.numpy as jnp
import ml_dtypes
import numpy as np
from jax import lax
from jax.experimental import pallas as pl
from jax.experimental.pallas import tpu as pltpu
from jax.sharding import PartitionSpec as P

NG = 80
SCREEN = 0.1
MESH = pl.DeviceIdType.MESH
ROWS = 104
BIG, SMALL = 7, 6


def row_of(a, x):
    return 8 * a + x if x < 8 else 80 + 2 * a + x - 8


def plane_of(source, x):
    return 8 * source + x if x < 8 else 64 + 2 * source + x - 8


def halves(table):
    table = np.asarray(table, np.float64)
    high = table.astype(np.float32).astype(ml_dtypes.bfloat16)
    low = (table - high.astype(np.float64)).astype(np.float32).astype(ml_dtypes.bfloat16)
    return np.stack([high, low])


def wave(k):
    k = np.where(k > NG // 2, k - NG, k)
    return (k * (2.0 * math.pi / NG)) ** 2


def complex_map(table):
    out = np.zeros((2, table.shape[0], 2, table.shape[1]))
    out[0, :, 0], out[1, :, 0] = table.real, -table.imag
    out[0, :, 1], out[1, :, 1] = table.imag, table.real
    return out


def tables():
    z = np.arange(NG)
    into = np.zeros((8, NG, 6, 128))
    back = np.zeros((6, 128, 8, NG))
    for r in range(8):
        for kz in range(40):
            g, j = divmod(kz, 8)
            angle = 2 * math.pi * (kz * z % NG) / NG
            weight = 1.0 if kz == 0 else 2.0
            into[r, :, g, j * 8 + r] = np.cos(angle)
            into[r, :, g, 64 + j * 8 + r] = -np.sin(angle)
            back[g, j * 8 + r, r] = weight * np.cos(angle)
            back[g, 64 + j * 8 + r, r] = -weight * np.sin(angle)
        sign = 1.0 - 2.0 * (z % 2)
        for lane in range(r, 128, 8):
            into[r, :, 5, lane] = sign
            back[5, lane, r] = sign
    along_y = np.zeros((2, ROWS, 112))
    for k in range(10):
        for a in range(10):
            angle = 2 * math.pi * (k * a % 10) / 10
            for x in range(10):
                along_y[0, row_of(k, x), row_of(a, x)] = math.cos(angle)
                along_y[1, row_of(k, x), row_of(a, x)] = math.sin(angle)
    along_x = np.zeros((2, NG, NG))
    k = np.arange(NG)
    for source in range(8):
        for x in range(10):
            angle = 2 * math.pi * (k * (10 * source + x) % NG) / NG
            along_x[0, :, plane_of(source, x)] = np.cos(angle)
            along_x[1, :, plane_of(source, x)] = np.sin(angle)
    along_x = along_x.reshape(160, NG)
    fine = np.zeros((12, 2, 128, 128))
    fine_back = np.zeros((12, 128, 2, 128))
    waves = np.zeros((56, 128))
    r = np.arange(8)
    for k1 in range(10):
        ky = k1 + 10 * np.arange(8)
        phase = 2 * math.pi * (r[:, None] * ky[None, :] % NG) / NG
        table = np.exp(-1j * phase)
        forward = [complex_map(table), complex_map(-1j * table)]
        inverse = [complex_map(np.conj(table).T), complex_map(1j * np.conj(table).T)]
        for part in range(2):
            for c in range(2):
                for d in range(2):
                    for j in range(8):
                        fine[k1, part, c * 64 + j * 8 : c * 64 + j * 8 + 8, d * 64 + j * 8 : d * 64 + j * 8 + 8] = forward[part][c, :, d]
                        fine_back[k1, c * 64 + j * 8 : c * 64 + j * 8 + 8, part, d * 64 + j * 8 : d * 64 + j * 8 + 8] = inverse[part][c, :, d]
                    last, at = 10 + k1 // 8, k1 % 8 * 16
                    fine[last, part, at + c * 8 : at + c * 8 + 8, at + d * 8 : at + d * 8 + 8] = forward[part][c, :, d]
                    fine_back[last, at + c * 8 : at + c * 8 + 8, part, at + d * 8 : at + d * 8 + 8] = inverse[part][c, :, d]
        for c in range(2):
            for kz in range(40):
                at = c * 64 + kz % 8 * 8
                waves[kz // 8 * 10 + k1, at : at + 8] = wave(ky) + wave(np.array(kz))
            at = k1 % 8 * 16 + c * 8
            waves[50 + k1 // 8, at : at + 8] = wave(ky) + wave(np.array(40))
    wave_x = np.broadcast_to(wave(k)[:, None], (NG, 128))
    return (
        halves(into.reshape(640, 768)),
        halves(along_y.reshape(2 * ROWS, 112)),
        halves(along_x),
        halves(fine.reshape(12, 256, 128)),
        halves(fine_back.reshape(12, 128, 256)),
        halves(along_x.T),
        halves(back.reshape(768, 640)),
        waves.astype(np.float32),
        np.ascontiguousarray(wave_x).astype(np.float32),
    )


def parts_of(value):
    high = value.astype(jnp.bfloat16)
    return high, (value - high.astype(jnp.float32)).astype(jnp.bfloat16)


def product(a, b):
    def dot(u, v):
        return jnp.dot(u, v, preferred_element_type=jnp.float32)

    return dot(a[0], b[0]) + (dot(a[1], b[0]) + dot(a[0], b[1]))


def table_of(ref):
    return ref[0], ref[1]


def kernel(
    pair_ref, bands_ref, into_c, along_y_c, along_x_c, fine_c, fine_back_c, across_c, back_c, waves_c, wave_x_c,
    out_ref,
    bands, packed, into_t, along_y_t, along_x_t, fine_t, fine_back_t, across_t, back_t, waves_t, wave_x_t,
    band_out, band_in, own, kept, given, taken,
    go_big, go_small, at_big, at_small, ret_big, ret_small, home_big, home_small,
    lines, lines_small, columns,
    load_sem, band_sem, share_sem,
    go_big_sem, go_small_sem, at_big_sem, at_small_sem, ret_big_sem, ret_small_sem, home_big_sem, home_small_sem,
):
    band = lax.axis_index("band")
    grid = lax.axis_index("grid")
    z_low, y_core = lax.div(band, 8), lax.rem(band, 8)
    x_at, z = lax.div(grid, 2), lax.rem(grid, 2) * 8 + lax.div(band, 8)

    def site(x, half):
        far = lax.rem(z_low + 4 + 8 * half, 16)
        return (lax.rem(far, 8) * 8 + y_core, x * 2 + lax.div(far, 8))

    behind = lax.rem(z + 12, 16)
    my_half = lax.div(behind, 8)

    def source(g):
        return (lax.rem(behind, 8) * 8 + y_core, g)

    def neighbour(step):
        return (lax.rem(band + step + 64, 64), grid)

    def remote(src, dst, send, recv, device):
        return pltpu.make_async_remote_copy(
            src_ref=src, dst_ref=dst, send_sem=send, recv_sem=recv, device_id=device, device_id_type=MESH
        )

    loads = [pltpu.make_async_copy(bands_ref, bands, load_sem.at[0])]
    constants = (
        (into_c, into_t), (along_y_c, along_y_t), (along_x_c, along_x_t), (fine_c, fine_t), (fine_back_c, fine_back_t),
        (across_c, across_t), (back_c, back_t), (waves_c, waves_t), (wave_x_c, wave_x_t),
    )
    for number, (src, dst) in enumerate(constants):
        loads.append(pltpu.make_async_copy(src, dst, load_sem.at[number + 1]))
    for load in loads:
        load.start()

    barrier = pltpu.get_barrier_semaphore()
    friends = [neighbour(step) for step in (1, 2, -1, -2)]
    friends += [site(x, half) for half in range(2) for x in range(4)]
    for friend in friends:
        pl.semaphore_signal(barrier, inc=1, device_id=friend, device_id_type=MESH)

    loads[0].wait()

    def pack(k, carry):
        for q in range(5):
            for a in range(10):
                lanes = pl.ds((a * 5 + q) * 128, 128)
                packed[k, q, pl.ds(8 * a, 8), :] = bands[k, 0:8, lanes]
                packed[k, q, pl.ds(80 + 2 * a, 2), :] = bands[k, 8:10, lanes]
            packed[k, q, pl.ds(100, 4), :] = jnp.zeros((4, 128), jnp.float32)
        return carry

    lax.fori_loop(0, 4, pack, 0)
    for p in range(2):
        band_out[p] = packed[pair_ref[0, p, 0, 0]]
        second = pair_ref[0, p, 0, 1].astype(jnp.float32)
        band_out[p, 0, pl.ds(100, 4), :] = jnp.full((4, 128), second, jnp.float32)

    pl.semaphore_wait(barrier, 12)
    shares = [
        remote(band_out.at[p], band_in.at[p], band_sem.at[0, p], band_sem.at[1, p], neighbour(p + 1)) for p in range(2)
    ]
    for share in shares:
        share.start()
    for load in loads[1:]:
        load.wait()

    lane = lax.broadcasted_iota(jnp.int32, (1, 128), 1)
    flip = jnp.where(lane < 64, 1.0, -1.0).astype(jnp.float32)
    real_lane = lax.rem(lax.div(lane, 8), 2) == 0
    slot_lane = lax.div(lane, 16)
    nothing = jnp.zeros((8, 128), jnp.float32)

    def places(p):
        for x in range(4):
            first = BIG if p == 0 else SMALL
            for j in range(13):
                big = (j < first) == (p == 0)
                yield 13 * x + j, x, big, j if j < first else j - first

    def targets(p):
        for x in range(4):
            yield x, True, p
            yield x, False, 1 - p

    def going(p, x, big, half):
        if big:
            return remote(go_big.at[p, x], at_big.at[grid], go_big_sem.at[p, x], at_big_sem.at[grid], site(x, half))
        return remote(go_small.at[p, x], at_small.at[grid], go_small_sem.at[p, x], at_small_sem.at[grid], site(x, half))

    def returning(g, big):
        if big:
            return remote(
                ret_big.at[g], home_big.at[my_half, x_at], ret_big_sem.at[g], home_big_sem.at[my_half, x_at], source(g)
            )
        return remote(
            ret_small.at[g], home_small.at[1 - my_half, x_at], ret_small_sem.at[g], home_small_sem.at[1 - my_half, x_at],
            source(g),
        )

    def forward(p):
        shares[p].wait_recv()
        wanted = band_in[p, 0, pl.ds(100, 1), :]
        density = []
        for q in range(5):
            mine = packed[3, q]
            for k in range(3):
                mine = jnp.where(wanted == float(k), packed[k, q], mine)
            own[p, q] = mine
            density.append(jnp.concatenate([band_in[p, q] * mine, nothing], axis=0))
        rows = product(parts_of(jnp.concatenate(density, axis=1)), table_of(into_t))
        both = product(table_of(along_y_t), parts_of(rows))
        tiles = []
        for g in range(5):
            span = slice(g * 128, g * 128 + 128)
            tiles.append(both[:ROWS, span] + flip * pltpu.roll(both[ROWS:, span], 64, 1))
        last = jnp.where(real_lane, both[:ROWS, 640:], -both[ROWS:, 640:])
        for tile, x, big, j in places(p):
            buffer, size = (go_big, BIG) if big else (go_small, SMALL)
            g, k = divmod(tile, 10)
            if g < 5:
                main = tiles[g][8 * k : 8 * k + 8]
                rest = tiles[g][80 + 2 * k : 82 + 2 * k]
            else:
                main = jnp.zeros((8, 128), jnp.float32)
                rest = jnp.zeros((2, 128), jnp.float32)
                for k1 in range(8 * k, min(8 * k + 8, 10)):
                    here = slot_lane == k1 - 8 * k
                    main = jnp.where(here, last[8 * k1 : 8 * k1 + 8], main)
                    rest = jnp.where(here, last[80 + 2 * k1 : 82 + 2 * k1], rest)
            buffer[p, x, pl.ds(8 * j, 8), :] = main
            buffer[p, x, pl.ds(8 * size + 2 * j, 2), :] = rest
        for x, big, half in targets(p):
            going(p, x, big, half).start()

    def middle(big):
        size = BIG if big else SMALL
        arrived, arrived_sem, sent = (at_big, at_big_sem, ret_big) if big else (at_small, at_small_sem, ret_small)
        buffer = lines if big else lines_small
        start = 13 * x_at + (6 if big else 7) * my_half
        for g in range(8):
            remote(arrived.at[g], arrived.at[g], arrived_sem.at[g], arrived_sem.at[g], source(g)).wait_recv()
        for j in range(size):
            for g in range(8):
                buffer[pl.ds(8 * g, 8), pl.ds(128 * j, 128)] = arrived[g, pl.ds(8 * j, 8), :]
                buffer[pl.ds(64 + 2 * g, 2), pl.ds(128 * j, 128)] = arrived[g, pl.ds(8 * size + 2 * j, 2), :]
        waved = product(table_of(along_x_t), parts_of(buffer[...]))
        ups, downs = [], []
        for j in range(size):
            span = slice(128 * j, 128 * j + 128)
            tile = start + j
            which = lax.rem(tile, 10) + 10 * lax.div(tile, 50)
            pair = jnp.concatenate([waved[:NG, span], waved[NG:, span]], axis=1)
            spectrum = product(parts_of(pair), (fine_t[0, which], fine_t[1, which]))
            total = wave_x_t[...] + waves_t[pl.ds(tile, 1), :] + SCREEN * SCREEN
            spectrum = spectrum * ((1.0 / NG**3) / total)
            pair = product(parts_of(spectrum), (fine_back_t[0, which], fine_back_t[1, which]))
            ups.append(pair[:, :128])
            downs.append(pair[:, 128:])
        stacked = jnp.concatenate([jnp.concatenate(ups, axis=1), jnp.concatenate(downs, axis=1)], axis=0)
        result = product(table_of(across_t), parts_of(stacked))
        for g in range(8):
            for j in range(size):
                span = slice(128 * j, 128 * j + 128)
                sent[g, pl.ds(8 * j, 8), :] = result[8 * g : 8 * g + 8, span]
                sent[g, pl.ds(8 * size + 2 * j, 2), :] = result[64 + 2 * g : 66 + 2 * g, span]
            returning(g, big).start()

    def giving(p, q):
        return remote(
            given.at[p, q], taken.at[p, q], share_sem.at[0, p, q], share_sem.at[1, p, q], neighbour(-p - 1)
        )

    def backward(p):
        for x, big, half in targets(p):
            home, home_sem = (home_big, home_big_sem) if big else (home_small, home_small_sem)
            remote(home.at[p, x], home.at[p, x], home_sem.at[p, x], home_sem.at[p, x], site(x, half)).wait_recv()
        for tile, x, big, j in places(p):
            home, size = (home_big, BIG) if big else (home_small, SMALL)
            main = home[p, x, pl.ds(8 * j, 8), :]
            rest = home[p, x, pl.ds(8 * size + 2 * j, 2), :]
            g, k = divmod(tile, 10)
            if g < 5:
                columns[pl.ds(8 * k, 8), pl.ds(128 * g, 128)] = main
                columns[pl.ds(80 + 2 * k, 2), pl.ds(128 * g, 128)] = rest
            else:
                for k1 in range(8 * k, min(8 * k + 8, 10)):
                    here = slot_lane == k1 - 8 * k
                    columns[pl.ds(8 * k1, 8), pl.ds(640, 128)] = jnp.where(here, main, 0.0)
                    columns[pl.ds(80 + 2 * k1, 2), pl.ds(640, 128)] = jnp.where(here, rest, 0.0)
        both = product(table_of(along_y_t), parts_of(columns[...]))
        tiles = []
        for g in range(5):
            span = slice(g * 128, g * 128 + 128)
            tiles.append(both[:ROWS, span] - flip * pltpu.roll(both[ROWS:, span], 64, 1))
        tiles.append(jnp.where(real_lane, both[:ROWS, 640:], -both[ROWS:, 640:]))
        rows = parts_of(jnp.concatenate([jnp.concatenate(tiles, axis=1), jnp.zeros((8, 768), jnp.float32)], axis=0))
        for q in range(5):
            span = pl.ds(128 * q, 128)
            potential = product(rows, (back_t[0, :, span], back_t[1, :, span]))[:ROWS]
            kept[p, q] = potential * band_in[p, q]
            given[p, q] = (potential * own[p, q])[:100]
            giving(p, q).start()

    columns[pl.ds(96, 16), :] = jnp.zeros((16, 768), jnp.float32)
    forward(0)
    forward(1)
    pl.when(my_half == 0)(lambda: middle(True))
    middle(False)
    pl.when(my_half == 1)(lambda: middle(True))
    backward(0)
    backward(1)

    seconds = [band_in[p, 0, pl.ds(100, 1), :] for p in range(2)]
    for q in range(5):
        for p in range(2):
            giving(p, q).wait_recv()
        for k in range(4):
            total = jnp.zeros((100, 128), jnp.float32)
            for p in range(2):
                total = total - jnp.where(seconds[p] == float(k), kept[p, q, pl.ds(0, 100), :], 0.0)
                total = total - jnp.where(pair_ref[0, p, 0, 0] == k, taken[p, q], 0.0)
            for a in range(10):
                lanes = pl.ds((a * 5 + q) * 128, 128)
                out_ref[k, 0:8, lanes] = total[8 * a : 8 * a + 8]
                out_ref[k, 8:10, lanes] = total[80 + 2 * a : 82 + 2 * a]

    for p in range(2):
        shares[p].wait_send()
        for x, big, half in targets(p):
            going(p, x, big, half).wait_send()
        for q in range(5):
            giving(p, q).wait_send()
    for g in range(8):
        returning(g, True).wait_send()
        returning(g, False).wait_send()


def body(bands, pair_list):
    constants = [jnp.asarray(table) for table in tables()]
    f32 = jnp.float32
    dma = pltpu.SemaphoreType.DMA
    scratch = [pltpu.VMEM((4, 10, 6400), f32), pltpu.VMEM((4, 5, ROWS, 128), f32)]
    scratch += [pltpu.VMEM(table.shape, table.dtype) for table in constants]
    scratch += [pltpu.VMEM((2, 5, ROWS, 128), f32)] * 4
    scratch += [pltpu.VMEM((2, 5, 100, 128), f32)] * 2
    big, small = 10 * BIG, 10 * SMALL
    scratch += [pltpu.VMEM((2, 4, big, 128), f32), pltpu.VMEM((2, 4, small, 128), f32)]
    scratch += [pltpu.VMEM((8, big, 128), f32), pltpu.VMEM((8, small, 128), f32)] * 2
    scratch += [pltpu.VMEM((2, 4, big, 128), f32), pltpu.VMEM((2, 4, small, 128), f32)]
    scratch += [pltpu.VMEM((NG, 128 * BIG), f32), pltpu.VMEM((NG, 128 * SMALL), f32), pltpu.VMEM((112, 768), f32)]
    scratch += [dma((10,)), dma((2, 2)), dma((2, 2, 5))]
    scratch += [dma((2, 4))] * 2 + [dma((8,))] * 4 + [dma((2, 4))] * 2
    return pl.pallas_call(
        kernel,
        out_shape=jax.ShapeDtypeStruct(bands.shape, f32),
        in_specs=[pl.BlockSpec(memory_space=pltpu.SMEM)] + [pl.BlockSpec(memory_space=pl.ANY)] * 10,
        out_specs=pl.BlockSpec(memory_space=pltpu.VMEM),
        scratch_shapes=scratch,
        compiler_params=pltpu.CompilerParams(collective_id=0, has_side_effects=True, vmem_limit_bytes=48 * 2**20),
        name="exchange",
    )(pair_list, bands, *constants)


def solution(mesh):
    in_specs = (P("band", "grid", None), P("band", None, None, None))
    out_specs = P("band", "grid", None)
    return jax.shard_map(body, mesh=mesh, in_specs=in_specs, out_specs=out_specs, check_vma=False)
```

profile of v0, /device:TPU:48, one launch (start us, length us, event | category | flops | bytes accessed | tf_op | source)
XLA Modules:
  0.0 94.0 jit_solution(9530465449686672118)
XLA Ops:
  0.0 0.0 copy-start.5
  0.0 0.0 copy-start.6
  0.0 0.0 copy-start.3
  0.0 0.0 copy-start
  0.0 0.0 copy-start.4
  0.0 0.0 copy-start.2
  0.0 0.0 copy-start.7
  0.1 2.8 %copy.12.bands_ref = f32[4,10,6400]{2,1,0:T(8,128)} copy(f32[4,10,6400]{2,0,1:T(4,128)} %param.11) | data formatting | bytes 2048000 | tf_op args[0]
  2.8 0.0 copy-done.5
  2.8 0.0 copy-done.6
  2.8 0.0 copy-done.3
  2.8 0.0 copy-done
  2.8 0.0 copy-done.4
  2.8 0.0 copy-done.2
  2.9 0.0 copy-done.7
  2.9 0.0 copy-start.1
  2.9 1.4 %copy-done.1 = bf16[2,12,256,128]{3,2,1,0:T(8,128)(2,1)S(1)} copy-done((bf16[2,12,256,128]{3,2,1,0:T(8,128)(2,1)S(1)}, bf16[2,12,256,128]{3,2,1,0:T(8,128)(2,1)}, u32[]{:S(2)}) %copy-start.1) | copy-done | bytes 1572888
  4.3 88.1 %exchange.1 = f32[4,10,6400]{2,1,0:T(8,128)S(1)} custom-call(s32[1,2,1,2]{3,2,1,0:T(1,128)S(1)} %copy-done.7, f32[4,10,6400]{2,1,0:T(8,128)} %copy.12.bands_ref, bf16[2,640,768]{2,1,0:T(8,128)(2,1)} %constant.18.clone.into_c, bf16[2,208,112]{2,1,0:T(8,128)(2,1)S(1)} %copy-done.2, bf16[2,160,80]{2,1,0:T(8,128)(2,1)S(1)} %copy-done.4, ...), custom_call_target="tpu_custom_call" | custom-call | tf_op jit(solution)/shard_map/exchange/pallas_call | solution.py:394
  92.3 1.6 %copy.13 = f32[4,10,6400]{2,0,1:T(4,128)} copy(f32[4,10,6400]{2,1,0:T(8,128)S(1)} %exchange.1) | data formatting | bytes 2048000 | tf_op jit(solution)/shard_map/exchange/pallas_call | solution.py:394
Async XLA Ops:
  0.0 2.8 %copy-start.5 = (f32[80,128]{1,0:T(8,128)S(1)}, f32[80,128]{1,0:T(8,128)}, u32[]{:S(2)}) copy-start(f32[80,128]{1,0:T(8,128)} %constant.26.clone.wave_x_c) | copy-start | bytes 122884
  0.0 2.8 %copy-start.6 = (f32[56,128]{1,0:T(8,128)S(1)}, f32[56,128]{1,0:T(8,128)}, u32[]{:S(2)}) copy-start(f32[56,128]{1,0:T(8,128)} %constant.25.clone.waves_c) | copy-start | bytes 86020
  0.0 2.8 %copy-start.3 = (bf16[2,80,160]{2,1,0:T(8,128)(2,1)S(1)}, bf16[2,80,160]{2,1,0:T(8,128)(2,1)}, u32[]{:S(2)}) copy-start(bf16[2,80,160]{2,1,0:T(8,128)(2,1)} %constant.23.clone.across_c) | copy-start | bytes 153604
  0.0 2.8 %copy-start = (bf16[2,12,128,256]{3,2,1,0:T(8,128)(2,1)S(1)}, bf16[2,12,128,256]{3,2,1,0:T(8,128)(2,1)}, u32[]{:S(2)}) copy-start(bf16[2,12,128,256]{3,2,1,0:T(8,128)(2,1)} %constant.22.clone.fine_back_c) | copy-start | bytes 4718596
  0.0 2.8 %copy-start.4 = (bf16[2,160,80]{2,1,0:T(8,128)(2,1)S(1)}, bf16[2,160,80]{2,1,0:T(8,128)(2,1)}, u32[]{:S(2)}) copy-start(bf16[2,160,80]{2,1,0:T(8,128)(2,1)} %constant.20.clone.along_x_c) | copy-start | bytes 153604
  0.0 2.8 %copy-start.2 = (bf16[2,208,112]{2,1,0:T(8,128)(2,1)S(1)}, bf16[2,208,112]{2,1,0:T(8,128)(2,1)}, u32[]{:S(2)}) copy-start(bf16[2,208,112]{2,1,0:T(8,128)(2,1)} %constant.19.clone.along_y_c) | copy-start | bytes 279556
  0.0 2.8 %copy-start.7 = (s32[1,2,1,2]{3,2,1,0:T(1,128)S(1)}, s32[1,2,1,2]{3,2,1,0:T(1,128)}, u32[]{:S(2)}) copy-start(s32[1,2,1,2]{3,2,1,0:T(1,128)} %pair_ref.1) | copy-start | bytes 52
  2.9 1.4 %copy-start.1 = (bf16[2,12,256,128]{3,2,1,0:T(8,128)(2,1)S(1)}, bf16[2,12,256,128]{3,2,1,0:T(8,128)(2,1)}, u32[]{:S(2)}) copy-start(bf16[2,12,256,128]{3,2,1,0:T(8,128)(2,1)} %constant.21.clone.fine_c) | copy-start | bytes 4718596
where the time goes:
time: 94.1 us; the launch traced here: 94 us
  Pallas kernels  88.1 us (94%)
  local copies, waits for them, and re-layouts  5.82 us (6%)
    pallas_call x1, Pallas kernels, body(): pl.pallas_call(kernel, out_shape=jax.ShapeDtypeStruct(bands.shape, f32),...  88.1 us
    unnamed x17, local copies, waits for them, and re-layouts  4.2 us

commit v1 on v0

--- a/solution.py
+++ b/solution.py
@@ -133,11 +133,11 @@
 def kernel(
     pair_ref, bands_ref, into_c, along_y_c, along_x_c, fine_c, fine_back_c, across_c, back_c, waves_c, wave_x_c,
     out_ref,
-    bands, packed, into_t, along_y_t, along_x_t, fine_t, fine_back_t, across_t, back_t, waves_t, wave_x_t,
-    band_out, band_in, own, kept, given, taken,
+    bands, staged, packed, into_t, along_y_t, along_x_t, fine_t, fine_back_t, across_t, back_t, waves_t, wave_x_t,
+    band_out, band_in, index_out, index_in, own, kept, given, taken,
     go_big, go_small, at_big, at_small, ret_big, ret_small, home_big, home_small,
     lines, lines_small, columns,
-    load_sem, band_sem, share_sem,
+    load_sem, band_sem, index_sem, share_sem,
     go_big_sem, go_small_sem, at_big_sem, at_small_sem, ret_big_sem, ret_small_sem, home_big_sem, home_small_sem,
 ):
     band = lax.axis_index("band")
@@ -181,27 +181,36 @@
 
     loads[0].wait()
 
+    def stage(t, carry):
+        lanes = pl.ds(pl.multiple_of(t * 128, 128), 128)
+        for x in range(10):
+            staged[pl.ds(pl.multiple_of(t * 40 + 4 * x, 4), 4), :] = bands[x, :, lanes]
+        return carry
+
+    lax.fori_loop(0, 50, stage, 0, unroll=5)
+
     def pack(k, carry):
         for q in range(5):
             for a in range(10):
-                lanes = pl.ds((a * 5 + q) * 128, 128)
-                packed[k, q, pl.ds(8 * a, 8), :] = bands[k, 0:8, lanes]
-                packed[k, q, pl.ds(80 + 2 * a, 2), :] = bands[k, 8:10, lanes]
+                first = (a * 5 + q) * 40 + k
+                packed[k, q, pl.ds(8 * a, 8), :] = staged[pl.ds(first, 8, stride=4), :]
+                packed[k, q, pl.ds(80 + 2 * a, 2), :] = staged[pl.ds(first + 32, 2, stride=4), :]
             packed[k, q, pl.ds(100, 4), :] = jnp.zeros((4, 128), jnp.float32)
         return carry
 
     lax.fori_loop(0, 4, pack, 0)
-    for p in range(2):
-        band_out[p] = packed[pair_ref[0, p, 0, 0]]
-        second = pair_ref[0, p, 0, 1].astype(jnp.float32)
-        band_out[p, 0, pl.ds(100, 4), :] = jnp.full((4, 128), second, jnp.float32)
+    band_out[0] = packed[pair_ref[0, 0, 0, 0]]
+    band_out[0, 0, pl.ds(100, 4), :] = jnp.full((4, 128), pair_ref[0, 0, 0, 1].astype(jnp.float32), jnp.float32)
+    index_out[...] = jnp.full((8, 128), pair_ref[0, 1, 0, 1].astype(jnp.float32), jnp.float32)
 
     pl.semaphore_wait(barrier, 12)
+    steps = (1, 2 - 4 * lax.rem(band, 2))
     shares = [
-        remote(band_out.at[p], band_in.at[p], band_sem.at[0, p], band_sem.at[1, p], neighbour(p + 1)) for p in range(2)
+        remote(band_out.at[p], band_in.at[p], band_sem.at[0, p], band_sem.at[1, p], neighbour(steps[p])) for p in range(2)
     ]
-    for share in shares:
-        share.start()
+    notice = remote(index_out, index_in, index_sem.at[0], index_sem.at[1], neighbour(2))
+    shares[0].start()
+    notice.start()
     for load in loads[1:]:
         load.wait()
 
@@ -210,6 +219,20 @@
     real_lane = lax.rem(lax.div(lane, 8), 2) == 0
     slot_lane = lax.div(lane, 16)
     nothing = jnp.zeros((8, 128), jnp.float32)
+
+    def chosen(index, q):
+        value = packed[3, q]
+        for k in range(3):
+            value = jnp.where(index == float(k), packed[k, q], value)
+        return value
+
+    def roles(p):
+        ours = jnp.full((1, 128), pair_ref[0, p, 0, 0].astype(jnp.float32), jnp.float32)
+        if p == 0:
+            return ours, band_in[0, 0, pl.ds(100, 1), :]
+        theirs = index_in[pl.ds(0, 1), :]
+        here = lax.rem(band, 2) == 0
+        return jnp.where(here, ours, theirs), jnp.where(here, theirs, ours)
 
     def places(p):
         for x in range(4):
@@ -240,12 +263,10 @@
 
     def forward(p):
         shares[p].wait_recv()
-        wanted = band_in[p, 0, pl.ds(100, 1), :]
+        wanted = roles(p)[1]
         density = []
         for q in range(5):
-            mine = packed[3, q]
-            for k in range(3):
-                mine = jnp.where(wanted == float(k), packed[k, q], mine)
+            mine = chosen(wanted, q)
             own[p, q] = mine
             density.append(jnp.concatenate([band_in[p, q] * mine, nothing], axis=0))
         rows = product(parts_of(jnp.concatenate(density, axis=1)), table_of(into_t))
@@ -273,13 +294,20 @@
         for x, big, half in targets(p):
             going(p, x, big, half).start()
 
+    def arrive(big):
+        arrived, arrived_sem = (at_big, at_big_sem) if big else (at_small, at_small_sem)
+        for g in range(8):
+            remote(arrived.at[g], arrived.at[g], arrived_sem.at[g], arrived_sem.at[g], source(g)).wait_recv()
+
+    def leave(big):
+        for g in range(8):
+            returning(g, big).start()
+
     def middle(big):
         size = BIG if big else SMALL
-        arrived, arrived_sem, sent = (at_big, at_big_sem, ret_big) if big else (at_small, at_small_sem, ret_small)
+        arrived, sent = (at_big, ret_big) if big else (at_small, ret_small)
         buffer = lines if big else lines_small
         start = 13 * x_at + (6 if big else 7) * my_half
-        for g in range(8):
-            remote(arrived.at[g], arrived.at[g], arrived_sem.at[g], arrived_sem.at[g], source(g)).wait_recv()
         for j in range(size):
             for g in range(8):
                 buffer[pl.ds(8 * g, 8), pl.ds(128 * j, 128)] = arrived[g, pl.ds(8 * j, 8), :]
@@ -304,11 +332,10 @@
                 span = slice(128 * j, 128 * j + 128)
                 sent[g, pl.ds(8 * j, 8), :] = result[8 * g : 8 * g + 8, span]
                 sent[g, pl.ds(8 * size + 2 * j, 2), :] = result[64 + 2 * g : 66 + 2 * g, span]
-            returning(g, big).start()
 
     def giving(p, q):
         return remote(
-            given.at[p, q], taken.at[p, q], share_sem.at[0, p, q], share_sem.at[1, p, q], neighbour(-p - 1)
+            given.at[p, q], taken.at[p, q], share_sem.at[0, p, q], share_sem.at[1, p, q], neighbour(-steps[p])
         )
 
     def backward(p):
@@ -343,28 +370,44 @@
             giving(p, q).start()
 
     columns[pl.ds(96, 16), :] = jnp.zeros((16, 768), jnp.float32)
+    def meet(first):
+        arrive(first)
+        middle(first)
+        arrive(not first)
+        leave(first)
+        middle(not first)
+        leave(not first)
+
     forward(0)
+    notice.wait_recv()
+    for q in range(5):
+        band_out[1, q] = chosen(roles(1)[0], q)
+    shares[1].start()
     forward(1)
-    pl.when(my_half == 0)(lambda: middle(True))
-    middle(False)
-    pl.when(my_half == 1)(lambda: middle(True))
+    pl.when(my_half == 0)(lambda: meet(True))
+    pl.when(my_half == 1)(lambda: meet(False))
     backward(0)
     backward(1)
 
-    seconds = [band_in[p, 0, pl.ds(100, 1), :] for p in range(2)]
+    moved, stayed = zip(*[roles(p) for p in range(2)])
     for q in range(5):
         for p in range(2):
             giving(p, q).wait_recv()
         for k in range(4):
             total = jnp.zeros((100, 128), jnp.float32)
             for p in range(2):
-                total = total - jnp.where(seconds[p] == float(k), kept[p, q, pl.ds(0, 100), :], 0.0)
-                total = total - jnp.where(pair_ref[0, p, 0, 0] == k, taken[p, q], 0.0)
+                total = total - jnp.where(stayed[p] == float(k), kept[p, q, pl.ds(0, 100), :], 0.0)
+                total = total - jnp.where(moved[p] == float(k), taken[p, q], 0.0)
             for a in range(10):
-                lanes = pl.ds((a * 5 + q) * 128, 128)
-                out_ref[k, 0:8, lanes] = total[8 * a : 8 * a + 8]
-                out_ref[k, 8:10, lanes] = total[80 + 2 * a : 82 + 2 * a]
-
+                first = (a * 5 + q) * 40 + k
+                staged[pl.ds(first, 8, stride=4), :] = total[8 * a : 8 * a + 8]
+                staged[pl.ds(first + 32, 2, stride=4), :] = total[80 + 2 * a : 82 + 2 * a]
+        for a in range(10):
+            t = a * 5 + q
+            for x in range(10):
+                out_ref[x, :, pl.ds(t * 128, 128)] = staged[pl.ds(t * 40 + 4 * x, 4), :]
+
+    notice.wait_send()
     for p in range(2):
         shares[p].wait_send()
         for x, big, half in targets(p):
@@ -380,26 +423,30 @@
     constants = [jnp.asarray(table) for table in tables()]
     f32 = jnp.float32
     dma = pltpu.SemaphoreType.DMA
-    scratch = [pltpu.VMEM((4, 10, 6400), f32), pltpu.VMEM((4, 5, ROWS, 128), f32)]
+    scratch = [pltpu.VMEM((10, 4, 6400), f32), pltpu.VMEM((2000, 128), f32), pltpu.VMEM((4, 5, ROWS, 128), f32)]
     scratch += [pltpu.VMEM(table.shape, table.dtype) for table in constants]
-    scratch += [pltpu.VMEM((2, 5, ROWS, 128), f32)] * 4
+    scratch += [pltpu.VMEM((2, 5, ROWS, 128), f32)] * 2
+    scratch += [pltpu.VMEM((8, 128), f32)] * 2
+    scratch += [pltpu.VMEM((2, 5, ROWS, 128), f32)] * 2
     scratch += [pltpu.VMEM((2, 5, 100, 128), f32)] * 2
     big, small = 10 * BIG, 10 * SMALL
     scratch += [pltpu.VMEM((2, 4, big, 128), f32), pltpu.VMEM((2, 4, small, 128), f32)]
     scratch += [pltpu.VMEM((8, big, 128), f32), pltpu.VMEM((8, small, 128), f32)] * 2
     scratch += [pltpu.VMEM((2, 4, big, 128), f32), pltpu.VMEM((2, 4, small, 128), f32)]
     scratch += [pltpu.VMEM((NG, 128 * BIG), f32), pltpu.VMEM((NG, 128 * SMALL), f32), pltpu.VMEM((112, 768), f32)]
-    scratch += [dma((10,)), dma((2, 2)), dma((2, 2, 5))]
+    scratch += [dma((10,)), dma((2, 2)), dma((2,)), dma((2, 2, 5))]
     scratch += [dma((2, 4))] * 2 + [dma((8,))] * 4 + [dma((2, 4))] * 2
-    return pl.pallas_call(
+    lines = bands.transpose(1, 0, 2)
+    action = pl.pallas_call(
         kernel,
-        out_shape=jax.ShapeDtypeStruct(bands.shape, f32),
+        out_shape=jax.ShapeDtypeStruct(lines.shape, f32),
         in_specs=[pl.BlockSpec(memory_space=pltpu.SMEM)] + [pl.BlockSpec(memory_space=pl.ANY)] * 10,
         out_specs=pl.BlockSpec(memory_space=pltpu.VMEM),
         scratch_shapes=scratch,
-        compiler_params=pltpu.CompilerParams(collective_id=0, has_side_effects=True, vmem_limit_bytes=48 * 2**20),
+        compiler_params=pltpu.CompilerParams(collective_id=0, has_side_effects=True, vmem_limit_bytes=62 * 2**20),
         name="exchange",
-    )(pair_list, bands, *constants)
+    )(pair_list, lines, *constants)
+    return action.transpose(1, 0, 2)
 
 
 def solution(mesh):

time: 94.1 us -> 91.3 us (0.970)
  the two profiles are of different devices: /device:TPU:48 before, /device:TPU:1 now
where the time goes in v1:
time: 91.3 us; the launch traced here: 91.1 us
  Pallas kernels  88.8 us (97%)
  local copies, waits for them, and re-layouts  2.24 us (2%)
    pallas_call x1, Pallas kernels, body(): pl.pallas_call(kernel, out_shape=jax.ShapeDtypeStruct(lines.shape, f32),...  88.8 us
    unnamed x1, local copies, waits for them, and re-layouts  2.24 us

profile of v1, /device:TPU:1, one launch (start us, length us, event | category | flops | bytes accessed | tf_op | source)
XLA Modules:
  0.0 91.1 jit_solution(15826463351478444899)
XLA Ops:
  0.0 88.8 %exchange.1 = f32[10,4,6400]{2,1,0:T(4,128)} custom-call(s32[1,2,1,2]{3,2,1,0:T(1,128)} %pair_ref.1, f32[10,4,6400]{2,1,0:T(4,128)} %bitcast.3, bf16[2,640,768]{2,1,0:T(8,128)(2,1)} %constant.18.clone.into_c, bf16[2,208,112]{2,1,0:T(8,128)(2,1)} %constant.19.clone.along_y_c, bf16[2,160,80]{2,1,0:T(8,128)(2,1)} %constant.20.clone.along_x_c, ...), custom_call_target="tpu_custom_call" | custom-call | tf_op jit(solution)/shard_map/exchange/pallas_call | solution.py:440
  88.9 2.2 %copy.13 = f32[4,10,6400]{2,0,1:T(4,128)} copy(f32[4,10,6400]{2,0,1:T(4,128)} %bitcast.2) | data formatting | bytes 2048000

commit v2 on v1

--- a/solution.py
+++ b/solution.py
@@ -370,13 +370,16 @@
             giving(p, q).start()
 
     columns[pl.ds(96, 16), :] = jnp.zeros((16, 768), jnp.float32)
+    later = lax.rem(band, 2) == 1
+
     def meet(first):
         arrive(first)
         middle(first)
         arrive(not first)
-        leave(first)
+        pl.when(jnp.logical_not(later))(lambda: leave(first))
         middle(not first)
         leave(not first)
+        pl.when(later)(lambda: leave(first))
 
     forward(0)
     notice.wait_recv()
@@ -386,8 +389,12 @@
     forward(1)
     pl.when(my_half == 0)(lambda: meet(True))
     pl.when(my_half == 1)(lambda: meet(False))
-    backward(0)
-    backward(1)
+    def finish(first):
+        backward(first)
+        backward(1 - first)
+
+    pl.when(later)(lambda: finish(1))
+    pl.when(jnp.logical_not(later))(lambda: finish(0))
 
     moved, stayed = zip(*[roles(p) for p in range(2)])
     for q in range(5):

time: 91.3 us -> 88.7 us (0.972)
  Pallas kernels: 88.8 us -> 86.3 us
    pallas_call x1, Pallas kernels: 88.8 us -> 86.3 us  [body(): pl.pallas_call(kernel, out_shape=jax.ShapeDtypeStruct(lines.shape, f32),...]
where the time goes in v2:
time: 88.7 us; the launch traced here: 88.5 us
  Pallas kernels  86.3 us (97%)
  local copies, waits for them, and re-layouts  2.24 us (3%)
    pallas_call x1, Pallas kernels, body(): pl.pallas_call(kernel, out_shape=jax.ShapeDtypeStruct(lines.shape, f32),...  86.3 us
    unnamed x1, local copies, waits for them, and re-layouts  2.24 us

profile of v2, /device:TPU:1, one launch (start us, length us, event | category | flops | bytes accessed | tf_op | source)
XLA Modules:
  0.0 88.5 jit_solution(7478279466584273136)
XLA Ops:
  0.0 86.3 %exchange.1 = f32[10,4,6400]{2,1,0:T(4,128)} custom-call(s32[1,2,1,2]{3,2,1,0:T(1,128)} %pair_ref.1, f32[10,4,6400]{2,1,0:T(4,128)} %bitcast.3, bf16[2,640,768]{2,1,0:T(8,128)(2,1)} %constant.18.clone.into_c, bf16[2,208,112]{2,1,0:T(8,128)(2,1)} %constant.19.clone.along_y_c, bf16[2,160,80]{2,1,0:T(8,128)(2,1)} %constant.20.clone.along_x_c, ...), custom_call_target="tpu_custom_call" | custom-call | tf_op jit(solution)/shard_map/exchange/pallas_call | solution.py:447
  86.3 2.2 %copy.13 = f32[4,10,6400]{2,0,1:T(4,128)} copy(f32[4,10,6400]{2,0,1:T(4,128)} %bitcast.2) | data formatting | bytes 2048000
